TPU v7x, 512 devices: a whole 4x4x16 slice. The times are simulated.
512 devices in a mesh: dp: 64 (over z, y_lo, core), tensor: 8 (over x, y_hi).
Axes of the slice: x: 4, y: 4 (y_hi: 2, y_lo: 2; y = y_hi * 2 + y_lo), z: 16, core: 2. Of those that a mesh axis runs over, the one named last changes fastest.
Arguments:
- activations: bfloat16 [98304, 2048], P('dp', 'tensor'), may hold values from -6 to 6
- out_grads: bfloat16 [98304, 2048], P('dp', 'tensor'), may hold values from -0.001953125 to 0.001953125
- left_stat: float32 [2048, 2048], P('dp', 'tensor'), may hold values from -1 to 11, as said below
- right_stat: float32 [2048, 2048], P('dp', 'tensor'), may hold values from -1 to 11, as said below
Outputs:
- left_new: float32 [2048, 2048], P('dp', 'tensor')
- right_new: float32 [2048, 2048], P('dp', 'tensor')
- update: float32 [2048, 2048], P('dp', 'tensor')
Inputs may be any that keep to these rules, and one draw needn't show every extreme that they name: `left_stat`: symmetric, with a positive diagonal. `right_stat`: symmetric, with a positive diagonal.
All inputs are finite; a program needn't handle non-finite values.
Results may differ from a plain program's by a relative error of at most 0.0012.
Values may be sent and summed in bfloat16 or wider, within the bound.
A program may use at most 64 MiB of HBM per device.

v0:
```python
import jax
import jax.numpy as jnp
from jax import lax
from jax.sharding import Mesh
from jax.sharding import PartitionSpec as P

TENSOR = ("tensor_0", "tensor_1")
DP = ("dp_0", "dp_1", "dp_2")
DP_TENSOR = ("dp_0", "dp_1", "dp_2", "tensor_0", "tensor_1")


def in_blocks(x, dim, length):
    lengths = x.shape
    blocks = x.reshape(*lengths[:dim], length, lengths[dim] // length, *lengths[dim + 1 :])
    return jnp.moveaxis(blocks, dim, 0)


def sum_at_owner(x, axis, dim):
    length = lax.axis_size(axis)
    blocks = lax.all_to_all(in_blocks(x, dim, length), axis, 0, 0, tiled=True)
    return jnp.sum(blocks, axis=0)


def in_order(blocks, dim):
    blocks = jnp.moveaxis(blocks, 0, dim)
    lengths = blocks.shape
    return blocks.reshape(*lengths[:dim], lengths[dim] * lengths[dim + 1], *lengths[dim + 2 :])


def gather_in_order(x, axes, turns):
    blocks = x
    for k in turns:
        blocks = lax.all_gather(blocks, axes[k])
    done = turns[::-1]
    back = [done.index(k) for k in range(len(axes))]
    blocks = blocks.transpose(*back, *range(len(axes), blocks.ndim))
    return blocks.reshape(-1, *x.shape)


def gathered_by_axis(x, axes, turns, dim):
    return in_order(gather_in_order(x, axes, turns), dim)


def side_by_side(arrays, axis, dim, along):
    both = jnp.concatenate(arrays, axis=along)
    result, at, gathered = (sum_at_owner(both, axis, dim), 0, [])
    for a in arrays:
        gathered.append(lax.slice_in_dim(result, at, at + a.shape[along], axis=along))
        at += a.shape[along]
    return tuple(gathered)


def by_axis(x, axes):
    for axis in axes:
        x = lax.psum(x, axis)
    return x


def sent_to_all(x, axis):
    length = lax.axis_size(axis)
    return lax.all_to_all(jnp.broadcast_to(x[None], (length, *x.shape)), axis, 0, 0, tiled=True)


def gather_directly(x, axis, dim):
    return in_order(sent_to_all(x, axis), dim)


def local(activations, out_grads, left_stat, right_stat):
    highest = lax.Precision.HIGHEST
    tensor_count = lax.axis_size(TENSOR)
    dp_count = lax.axis_size(DP)
    col_count = out_grads.shape[1]
    full_order = col_count * tensor_count
    row_count = full_order // dp_count
    grad_terms = lax.dot_general(
        lax.all_gather(activations, TENSOR, axis=1, tiled=True),
        out_grads,
        (((0,), (0,)), ((), ())),
        preferred_element_type=jnp.float32,
    )
    grad_block = sum_at_owner(grad_terms, DP, 0)
    grad_cols = gathered_by_axis(grad_block, DP, (1, 0, 2), 0)
    left_part = lax.dot_general(
        grad_block,
        grad_cols,
        (((1,), (1,)), ((), ())),
        precision=highest,
        preferred_element_type=jnp.float32,
    )
    dp_place = lax.axis_index(DP)
    row_start = dp_place * row_count
    tensor_rows = lax.all_to_all(grad_cols, TENSOR, split_axis=0, concat_axis=1, tiled=True)
    strip_cols = lax.dynamic_slice_in_dim(tensor_rows, row_start, row_count, 1)
    right_part = lax.dot_general(
        strip_cols,
        tensor_rows,
        (((0,), (0,)), ((), ())),
        precision=highest,
        preferred_element_type=jnp.float32,
    )
    left_sum, right_sum = side_by_side((left_part, right_part), TENSOR, 1, 0)
    left_new = 0.9 * left_stat + 0.1 * left_sum
    right_new = 0.9 * right_stat + 0.1 * right_sum
    left_sq = jnp.sum(left_new * left_new)
    right_sq = jnp.sum(right_new * right_new)
    grad_sq = jnp.sum(grad_block * grad_block)
    left_total, right_total, grad_total = (
        by_axis(left_sq, DP_TENSOR),
        by_axis(right_sq, DP_TENSOR),
        by_axis(grad_sq, DP_TENSOR),
    )
    left_scale = jnp.sqrt(left_total / full_order + 1e-06)
    right_scale = jnp.sqrt(right_total / full_order + 1e-06)
    left_whole = gather_directly(left_new, TENSOR, 1)
    left_product = jnp.dot(
        left_whole, grad_cols, precision=highest, preferred_element_type=jnp.float32
    )
    pre_left = 5.0 * grad_block - left_product / left_scale
    pre_rows = gather_directly(pre_left, TENSOR, 1)
    right_product = jnp.dot(
        pre_rows,
        lax.all_gather(right_new.astype(jnp.bfloat16), DP, axis=0, tiled=True).astype(jnp.float32),
        precision=highest,
        preferred_element_type=jnp.float32,
    )
    pre_block = 5.0 * pre_left - right_product / right_scale
    pre_sq = jnp.sum(pre_block * pre_block)
    pre_total = by_axis(pre_sq, DP_TENSOR)
    factor = jnp.sqrt(grad_total + 1e-06) / jnp.sqrt(pre_total + 1e-06)
    return (left_new, right_new, pre_block * factor)


def solution(mesh):
    finer = Mesh(
        mesh.devices.reshape(16, 2, 2, 4, 2), ("dp_0", "dp_1", "dp_2", "tensor_0", "tensor_1")
    )
    placed = (P(DP, TENSOR), P(DP, TENSOR), P(DP, TENSOR), P(DP, TENSOR))
    return jax.shard_map(
        local,
        mesh=finer,
        in_specs=placed,
        out_specs=(P(DP, TENSOR), P(DP, TENSOR), P(DP, TENSOR)),
        check_vma=False,
    )
```

profile of v0, /device:TPU:16, one launch (start us, length us, event | category | flops | bytes accessed | tf_op | source)
XLA Modules:
  0.0 582.7 jit_solution(15723450914595324753)
XLA Ops:
  8.0 119.7 %all-gather.8.cloned.1.call-done = bf16[1536,2048]{1,0:T(8,128)(2,1)} async-done(((bf16[1536,256]{1,0:T(8,128)(2,1)}), bf16[1536,2048]{1,0:T(8,128)(2,1)}) %all-gather.8.cloned.1.call-update) | async-done | bytes 6291472 | tf_op jit(solution)/shard_map/all_gather | solution.py:76
  127.6 4.7 fusion.10
  132.4 115.6 %all_to_all.39 = f32[64,32,256]{2,1,0:T(8,128)S(1)} all-to-all(f32[64,32,256]{2,1,0:T(8,128)S(1)} %bitcast.35), channel_id=1, replica_groups=mesh['dp_0'=16,'dp_1'=2,'dp_2'=2,'tensor_0'=4,'tensor_1'=2] {'dp_0','dp_..., dimensions={0} | all-to-all | bytes 4194304 | tf_op jit(solution)/shard_map/all_to_all | solution.py:20
  248.1 4.7 all-gather
  252.9 61.7 %all-gather.12.cloned.1.call-done = f32[32,32,256]{2,1,0:T(8,128)} async-done(((f32[2,32,256]{2,1,0:T(8,128)}), f32[32,32,256]{2,1,0:T(8,128)}) %all-gather.12.cloned.1.call-update) | async-done | bytes 1048592 | tf_op jit(solution)/shard_map/all_gather | solution.py:33
  314.6 20.0 %all-gather.14.cloned.1.call-done = f32[32,2,32,256]{3,2,1,0:T(8,128)} async-done(((f32[16,2,32,256]{3,2,1,0:T(8,128)}), f32[32,2,32,256]{3,2,1,0:T(8,128)}) %all-gather.14.cloned.1.call-update) | async-done | bytes 2097168 | tf_op jit(solution)/shard_map/all_gather | solution.py:33
  334.6 3.2 copy.11
  337.8 7.2 %all-to-all-start.1 = ((f32[8,256,256]{2,1,0:T(8,128)}), f32[8,256,256]{2,1,0:T(8,128)S(1)}, u32[]{:S(2)}, u32[]{:S(2)}) async-start(f32[8,256,256]{2,1,0:T(8,128)} %bitcast.7), calls=%async_computation.1 | async-start | bytes 4194304 | tf_op jit(solution)/shard_map/all_to_all | solution.py:92
  345.0 3.6 fusion.11
  348.7 27.0 %all-to-all-done.1 = f32[8,256,256]{2,1,0:T(8,128)S(1)} async-done(((f32[8,256,256]{2,1,0:T(8,128)}), f32[8,256,256]{2,1,0:T(8,128)S(1)}, u32[]{:S(2)}, u32[]{:S(2)}) %all-to-all-start.1) | async-done | bytes 2097184 | tf_op jit(solution)/shard_map/all_to_all | solution.py:92
  375.6 1.3 copy-done.1
  376.9 1.9 copy.13
  378.9 2.0 fusion.4
  381.0 13.0 %all_to_all.40 = f32[8,64,256]{2,1,0:T(8,128)S(1)} all-to-all(f32[8,64,256]{2,1,0:T(8,128)S(1)} %bitcast.37), channel_id=1, replica_groups=mesh['dp_0'=16,'dp_1'=2,'dp_2'=2,'tensor_0'=4,'tensor_1'=2] {'tensor_0',..., dimensions={0} | all-to-all | bytes 1048576 | tf_op jit(solution)/shard_map/all_to_all | solution.py:20
  394.0 1.2 fusion.7
  395.3 0.7 broadcast_in_dim.4
  396.0 5.6 all-to-all-start.3
  402.3 32.0 %all-reduce.1 = (f32[]{:T(128)}, f32[]{:T(128)}) all-reduce(f32[]{:T(128)} %get-tuple-element.27, f32[]{:T(128)} %multiply_reduce_fusion.2), channel_id=1, replica_groups=mesh['dp_0'=16,'dp_1'=2,'dp_2'=2,'tensor_0'=4,'tensor_1'=2] {'dp_0'}, use_global_device_ids=true, to_apply=%region_3.0 | all-reduce | flops 2 | bytes 16 | tf_op jit(solution)/shard_map/psum | solution.py:55
  434.3 5.6 all-reduce.9
  439.9 3.2 all-reduce.7
  443.1 11.1 %all-reduce.3 = (f32[]{:T(128)}, f32[]{:T(128)}) all-reduce(f32[]{:T(128)} %get-tuple-element.17, f32[]{:T(128)} %get-tuple-element.18), channel_id=1, replica_groups=mesh['dp_0'=16,'dp_1'=2,'dp_2'=2,'tensor_0'=4,'tensor_1'=2] {'tensor_0'}, use_global_device_ids=true, to_apply=%region_6.0 | all-reduce | flops 2 | bytes 16 | tf_op jit(solution)/shard_map/psum | solution.py:55
  454.2 7.1 %all-reduce.5 = (f32[]{:T(128)}, f32[]{:T(128)}) all-reduce(f32[]{:T(128)} %get-tuple-element.9, f32[]{:T(128)} %get-tuple-element.10), channel_id=1, replica_groups=mesh['dp_0'=16,'dp_1'=2,'dp_2'=2,'tensor_0'=4,'tensor_1'=2] {'tensor_1'}, use_global_device_ids=true, to_apply=%region_7.0 | all-reduce | flops 2 | bytes 16 | tf_op jit(solution)/shard_map/psum | solution.py:55
  462.1 2.7 fusion.1
  465.5 5.1 all-to-all-start.4
  471.8 4.9 all-to-all-done.4
  476.8 38.5 %all-gather.10.cloned.1.call-done = bf16[2048,256]{1,0:T(8,128)(2,1)} async-done(((bf16[32,256]{1,0:T(8,128)(2,1)}), bf16[2048,256]{1,0:T(8,128)(2,1)}) %all-gather.10.cloned.1.call-update) | async-done | bytes 1048592 | tf_op jit(solution)/shard_map/all_gather | solution.py:122
  515.3 2.4 multiply_reduce_fusion
  517.7 29.6 %all-reduce = (f32[]{:T(128)}, f32[]{:T(128)}) all-reduce(f32[]{:T(128)} %multiply_reduce_fusion.1, f32[]{:T(128)} %get-tuple-element.29), channel_id=1, replica_groups=mesh['dp_0'=16,'dp_1'=2,'dp_2'=2,'tensor_0'=4,'tensor_1'=2] {'dp_0'}, use_global_device_ids=true, to_apply=%region_15.0 | all-reduce | flops 2 | bytes 16 | tf_op jit(solution)/shard_map/psum | solution.py:55
  547.4 5.6 all-reduce.8
  553.0 3.1 all-reduce.6
  556.1 11.2 %all-reduce.2 = (f32[]{:T(128)}, f32[]{:T(128)}) all-reduce(f32[]{:T(128)} %get-tuple-element.15, f32[]{:T(128)} %get-tuple-element.16), channel_id=1, replica_groups=mesh['dp_0'=16,'dp_1'=2,'dp_2'=2,'tensor_0'=4,'tensor_1'=2] {'tensor_0'}, use_global_device_ids=true, to_apply=%region_18.0 | all-reduce | flops 2 | bytes 16 | tf_op jit(solution)/shard_map/psum | solution.py:55
  567.2 7.1 %all-reduce.4 = (f32[]{:T(128)}, f32[]{:T(128)}) all-reduce(f32[]{:T(128)} %get-tuple-element.7, f32[]{:T(128)} %get-tuple-element.8), channel_id=1, replica_groups=mesh['dp_0'=16,'dp_1'=2,'dp_2'=2,'tensor_0'=4,'tensor_1'=2] {'tensor_1'}, use_global_device_ids=true, to_apply=%region_19.0 | all-reduce | flops 2 | bytes 16 | tf_op jit(solution)/shard_map/psum | solution.py:55
  (30 shorter events, 3.7 us)
Async XLA Ops:
  7.2 120.5 %copy-start = (bf16[1536,256]{1,0:T(8,128)(2,1)S(1)}, bf16[1536,256]{1,0:T(8,128)(2,1)}, u32[]{:S(2)}) copy-start(bf16[1536,256]{1,0:T(8,128)(2,1)} %param.5) | copy-start | bytes 2359300
  7.2 120.4 %all-gather.8.cloned.1.call-start = ((), (), s32[]{:S(2)}) async-start(), calls=%async_computation.5 | async-start | bytes 7077888 | tf_op jit(solution)/shard_map/all_gather | solution.py:76
  7.9 306.7 %all-gather.12.cloned.1.call-start = ((), (), s32[]{:S(2)}) async-start(), calls=%async_computation.7 | async-start | bytes 1114112 | tf_op jit(solution)/shard_map/all_gather | solution.py:33
  252.8 81.8 %all-gather.14.cloned.1.call-start = ((), (), s32[]{:S(2)}) async-start(), calls=%async_computation.8 | async-start | bytes 3145728 | tf_op jit(solution)/shard_map/all_gather | solution.py:33
  337.8 37.8 %all-to-all-start.1 = ((f32[8,256,256]{2,1,0:T(8,128)}), f32[8,256,256]{2,1,0:T(8,128)S(1)}, u32[]{:S(2)}, u32[]{:S(2)}) async-start(f32[8,256,256]{2,1,0:T(8,128)} %bitcast.7), calls=%async_computation.1 | async-start | bytes 4194304 | tf_op jit(solution)/shard_map/all_to_all | solution.py:92
  345.0 170.2 %all-gather.10.cloned.1.call-start = ((), (), s32[]{:S(2)}) async-start(), calls=%async_computation.6 | async-start | bytes 1064960 | tf_op jit(solution)/shard_map/all_gather | solution.py:122
  375.6 1.3 copy-start.1
  380.9 13.1 %copy-start.4 = (f32[32,256]{1,0:T(8,128)S(1)}, f32[32,256]{1,0:T(8,128)}, u32[]{:S(2)}) copy-start(f32[32,256]{1,0:T(8,128)} %param.7) | copy-start | bytes 98308
  380.9 13.1 %copy-start.5 = (f32[32,256]{1,0:T(8,128)S(1)}, f32[32,256]{1,0:T(8,128)}, u32[]{:S(2)}) copy-start(f32[32,256]{1,0:T(8,128)} %param.6) | copy-start | bytes 98308
  395.2 70.3 %copy-start.2 = (f32[32,256]{1,0:T(8,128)}, f32[32,256]{1,0:T(8,128)S(1)}, u32[]{:S(2)}) copy-start(f32[32,256]{1,0:T(8,128)S(1)} %get-tuple-element.28) | copy-start | bytes 98308
  395.2 70.3 %copy-start.3 = (f32[32,256]{1,0:T(8,128)}, f32[32,256]{1,0:T(8,128)S(1)}, u32[]{:S(2)}) copy-start(f32[32,256]{1,0:T(8,128)S(1)} %get-tuple-element.24) | copy-start | bytes 98308
  396.0 66.1 %all-to-all-start.3 = ((f32[8,32,256]{2,1,0:T(8,128)}), f32[8,32,256]{2,1,0:T(8,128)S(1)}, u32[]{:S(2)}, u32[]{:S(2)}) async-start(f32[8,32,256]{2,1,0:T(8,128)} %broadcast_in_dim.4), calls=%async_computation.3 | async-start | bytes 524288 | tf_op jit(solution)/shard_map/all_to_all | solution.py:61
  465.5 11.2 %all-to-all-start.4 = ((f32[8,32,256]{2,1,0:T(8,128)}), f32[8,32,256]{2,1,0:T(8,128)S(1)}, u32[]{:S(2)}, u32[]{:S(2)}) async-start(f32[8,32,256]{2,1,0:T(8,128)} %broadcast_in_dim.5), calls=%async_computation.4 | async-start | bytes 524288 | tf_op jit(solution)/shard_map/all_to_all | solution.py:61
Sparse Core Ops, SparseCore 0:
  11.1 116.5 all-gather.7
  253.0 61.5 all-gather.11
  316.7 17.9 all-gather.13
  395.4 119.8 all-gather.9
where the time goes:
time: 584 us; the launch traced here: 583 us
  waiting for transfers between devices  273 us (47%)
  blocking collectives  249 us (43%)
  starting transfers between devices  18.1 us (3%)
  between operations  16.5 us (3%)
  matrix products  15.5 us (3%)
  local copies, waits for them, and re-layouts  7.96 us (1%)
    all_to_all x2, blocking collectives, sum_at_owner(): blocks = lax.all_to_all(in_blocks(x, dim, length), axis, 0, 0, tiled=True)  129 us
    all_gather x1, waiting for transfers between devices, local(): lax.all_gather(activations, TENSOR, axis=1, tiled=True)  120 us
    psum x10, blocking collectives, by_axis(): x = lax.psum(x, axis)  116 us
    all_gather x2, waiting for transfers between devices, gather_in_order(): blocks = lax.all_gather(blocks, axes[k])  81.7 us
    all_gather x1, waiting for transfers between devices, local(): lax.all_gather(right_new.astype(jnp.bfloat16), DP, axis=0, tiled=True)  38.5 us
    all_to_all x1, waiting for transfers between devices, local(): lax.all_to_all(grad_cols, TENSOR, split_axis=0, concat_axis=1, tiled=True)  27 us
  transfers between devices with their start and end apart: 7, of which 6 were waited for; matrix products, arithmetic and copies ran while one was open for 2% of the time, Pallas kernels for 0%

commit v1 on v0

--- a/solution.py
+++ b/solution.py
@@ -89,7 +89,12 @@
     )
     dp_place = lax.axis_index(DP)
     row_start = dp_place * row_count
-    tensor_rows = lax.all_to_all(grad_cols, TENSOR, split_axis=0, concat_axis=1, tiled=True)
+    tensor_rows = jnp.concatenate(
+        lax.all_to_all(
+            jnp.stack(jnp.split(grad_cols, lax.axis_size(TENSOR), axis=0)), TENSOR, 0, 0
+        ),
+        axis=1,
+    )
     strip_cols = lax.dynamic_slice_in_dim(tensor_rows, row_start, row_count, 1)
     right_part = lax.dot_general(
         strip_cols,

time: 584 us -> 590 us (1.010)
  the two profiles are of different devices: /device:TPU:16 before, /device:TPU:8 now
where the time goes in v1:
time: 590 us; the launch traced here: 589 us
  waiting for transfers between devices  277 us (47%)
  blocking collectives  250 us (42%)
  between operations  16.6 us (3%)
  local copies, waits for them, and re-layouts  13.9 us (2%)
  starting transfers between devices  13.9 us (2%)
  matrix products  13.9 us (2%)
    all_to_all x2, blocking collectives, sum_at_owner(): blocks = lax.all_to_all(in_blocks(x, dim, length), axis, 0, 0, tiled=True)  129 us
    all_gather x1, waiting for transfers between devices, local(): lax.all_gather(activations, TENSOR, axis=1, tiled=True)  121 us
    psum x10, blocking collectives, by_axis(): x = lax.psum(x, axis)  116 us
    all_gather x2, waiting for transfers between devices, gather_in_order(): blocks = lax.all_gather(blocks, axes[k])  80.7 us
    all_gather x1, waiting for transfers between devices, local(): lax.all_gather(right_new.astype(jnp.bfloat16), DP, axis=0, tiled=True)  39.3 us
    all_to_all x1, waiting for transfers between devices, local(): lax.all_to_all(jnp.stack(jnp.split(grad_cols, lax.axis_size(TENSOR), axis...  28.2 us
  transfers between devices with their start and end apart: 7, of which 6 were waited for; matrix products, arithmetic and copies ran while one was open for 1% of the time, Pallas kernels for 0%

profile of v1, /device:TPU:8, one launch (start us, length us, event | category | flops | bytes accessed | tf_op | source)
XLA Modules:
  0.0 589.4 jit_solution(15135091162974240539)
XLA Ops:
  8.0 121.3 %all-gather.8.cloned.1.call-done = bf16[1536,2048]{1,0:T(8,128)(2,1)} async-done(((bf16[1536,256]{1,0:T(8,128)(2,1)}), bf16[1536,2048]{1,0:T(8,128)(2,1)}) %all-gather.8.cloned.1.call-update) | async-done | bytes 6291472 | tf_op jit(solution)/shard_map/all_gather | solution.py:76
  129.3 4.7 fusion.11
  134.1 115.0 %all_to_all.25 = f32[64,32,256]{2,1,0:T(8,128)S(1)} all-to-all(f32[64,32,256]{2,1,0:T(8,128)S(1)} %bitcast.44), channel_id=1, replica_groups=mesh['dp_0'=16,'dp_1'=2,'dp_2'=2,'tensor_0'=4,'tensor_1'=2] {'dp_0','dp_..., dimensions={0} | all-to-all | bytes 4194304 | tf_op jit(solution)/shard_map/all_to_all | solution.py:20
  249.2 4.7 all-gather
  254.0 60.7 %all-gather.12.cloned.1.call-done = f32[32,32,256]{2,1,0:T(8,128)} async-done(((f32[2,32,256]{2,1,0:T(8,128)}), f32[32,32,256]{2,1,0:T(8,128)}) %all-gather.12.cloned.1.call-update) | async-done | bytes 1048592 | tf_op jit(solution)/shard_map/all_gather | solution.py:33
  314.7 20.0 %all-gather.14.cloned.1.call-done = f32[32,2,32,256]{3,2,1,0:T(8,128)} async-done(((f32[16,2,32,256]{3,2,1,0:T(8,128)}), f32[32,2,32,256]{3,2,1,0:T(8,128)}) %all-gather.14.cloned.1.call-update) | async-done | bytes 2097168 | tf_op jit(solution)/shard_map/all_gather | solution.py:33
  334.7 1.6 fusion.10
  342.4 5.8 all-to-all-start.1
  348.3 1.7 copy.18
  350.0 2.0 fusion.12
  352.0 28.2 %all-to-all-done.1 = f32[8,256,256]{2,1,0:T(8,128)} async-done(((f32[8,256,256]{2,1,0:T(8,128)}), f32[8,256,256]{2,1,0:T(8,128)}, u32[]{:S(2)}, u32[]{:S(2)}) %all-to-all-start.1) | async-done | bytes 2097184 | tf_op jit(solution)/shard_map/all_to_all | solution.py:93
  380.2 2.9 copy.27
  383.1 3.6 fusion.4
  386.9 14.0 %all_to_all.26 = f32[8,64,256]{2,1,0:T(8,128)S(1)} all-to-all(f32[8,64,256]{2,1,0:T(8,128)S(1)} %bitcast.46), channel_id=1, replica_groups=mesh['dp_0'=16,'dp_1'=2,'dp_2'=2,'tensor_0'=4,'tensor_1'=2] {'tensor_0',..., dimensions={0} | all-to-all | bytes 1048576 | tf_op jit(solution)/shard_map/all_to_all | solution.py:20
  400.9 2.0 fusion.7
  403.7 3.4 all-to-all-start.3
  407.7 31.9 %all-reduce.1 = (f32[]{:T(128)}, f32[]{:T(128)}) all-reduce(f32[]{:T(128)} %get-tuple-element.35, f32[]{:T(128)} %multiply_reduce_fusion.2), channel_id=1, replica_groups=mesh['dp_0'=16,'dp_1'=2,'dp_2'=2,'tensor_0'=4,'tensor_1'=2] {'dp_0'}, use_global_device_ids=true, to_apply=%region_3.0 | all-reduce | flops 2 | bytes 16 | tf_op jit(solution)/shard_map/psum | solution.py:55
  439.7 5.6 all-reduce.9
  445.3 3.1 all-reduce.7
  448.4 11.6 %all-reduce.3 = (f32[]{:T(128)}, f32[]{:T(128)}) all-reduce(f32[]{:T(128)} %get-tuple-element.17, f32[]{:T(128)} %get-tuple-element.18), channel_id=1, replica_groups=mesh['dp_0'=16,'dp_1'=2,'dp_2'=2,'tensor_0'=4,'tensor_1'=2] {'tensor_0'}, use_global_device_ids=true, to_apply=%region_6.0 | all-reduce | flops 2 | bytes 16 | tf_op jit(solution)/shard_map/psum | solution.py:55
  459.9 7.1 %all-reduce.5 = (f32[]{:T(128)}, f32[]{:T(128)}) all-reduce(f32[]{:T(128)} %get-tuple-element.9, f32[]{:T(128)} %get-tuple-element.10), channel_id=1, replica_groups=mesh['dp_0'=16,'dp_1'=2,'dp_2'=2,'tensor_0'=4,'tensor_1'=2] {'tensor_1'}, use_global_device_ids=true, to_apply=%region_7.0 | all-reduce | flops 2 | bytes 16 | tf_op jit(solution)/shard_map/psum | solution.py:55
  467.7 1.1 fusion.1
  468.8 0.7 broadcast_in_dim.5
  469.6 4.6 all-to-all-start.4
  475.5 7.2 %all-to-all-done.4 = f32[8,32,256]{2,1,0:T(8,128)S(1)} async-done(((f32[8,32,256]{2,1,0:T(8,128)}), f32[8,32,256]{2,1,0:T(8,128)S(1)}, u32[]{:S(2)}, u32[]{:S(2)}) %all-to-all-start.4) | async-done | bytes 262176 | tf_op jit(solution)/shard_map/all_to_all | solution.py:61
  482.6 39.3 %all-gather.10.cloned.1.call-done = bf16[2048,256]{1,0:T(8,128)(2,1)} async-done(((bf16[32,256]{1,0:T(8,128)(2,1)}), bf16[2048,256]{1,0:T(8,128)(2,1)}) %all-gather.10.cloned.1.call-update) | async-done | bytes 1048592 | tf_op jit(solution)/shard_map/all_gather | solution.py:127
  522.0 2.4 multiply_reduce_fusion
  524.4 29.7 %all-reduce = (f32[]{:T(128)}, f32[]{:T(128)}) all-reduce(f32[]{:T(128)} %multiply_reduce_fusion.1, f32[]{:T(128)} %get-tuple-element.37), channel_id=1, replica_groups=mesh['dp_0'=16,'dp_1'=2,'dp_2'=2,'tensor_0'=4,'tensor_1'=2] {'dp_0'}, use_global_device_ids=true, to_apply=%region_15.0 | all-reduce | flops 2 | bytes 16 | tf_op jit(solution)/shard_map/psum | solution.py:55
  554.1 5.6 all-reduce.8
  559.8 3.1 all-reduce.6
  562.9 11.1 %all-reduce.2 = (f32[]{:T(128)}, f32[]{:T(128)}) all-reduce(f32[]{:T(128)} %get-tuple-element.15, f32[]{:T(128)} %get-tuple-element.16), channel_id=1, replica_groups=mesh['dp_0'=16,'dp_1'=2,'dp_2'=2,'tensor_0'=4,'tensor_1'=2] {'tensor_0'}, use_global_device_ids=true, to_apply=%region_18.0 | all-reduce | flops 2 | bytes 16 | tf_op jit(solution)/shard_map/psum | solution.py:55
  573.9 7.1 %all-reduce.4 = (f32[]{:T(128)}, f32[]{:T(128)}) all-reduce(f32[]{:T(128)} %get-tuple-element.7, f32[]{:T(128)} %get-tuple-element.8), channel_id=1, replica_groups=mesh['dp_0'=16,'dp_1'=2,'dp_2'=2,'tensor_0'=4,'tensor_1'=2] {'tensor_1'}, use_global_device_ids=true, to_apply=%region_19.0 | all-reduce | flops 2 | bytes 16 | tf_op jit(solution)/shard_map/psum | solution.py:55
  (43 shorter events, 9.7 us)
Async XLA Ops:
  7.2 122.1 %copy-start = (bf16[1536,256]{1,0:T(8,128)(2,1)S(1)}, bf16[1536,256]{1,0:T(8,128)(2,1)}, u32[]{:S(2)}) copy-start(bf16[1536,256]{1,0:T(8,128)(2,1)} %param.5) | copy-start | bytes 2359300
  7.2 122.1 %all-gather.8.cloned.1.call-start = ((), (), s32[]{:S(2)}) async-start(), calls=%async_computation.5 | async-start | bytes 7077888 | tf_op jit(solution)/shard_map/all_gather | solution.py:76
  7.9 306.8 %all-gather.12.cloned.1.call-start = ((), (), s32[]{:S(2)}) async-start(), calls=%async_computation.7 | async-start | bytes 1114112 | tf_op jit(solution)/shard_map/all_gather | solution.py:33
  253.9 80.8 %all-gather.14.cloned.1.call-start = ((), (), s32[]{:S(2)}) async-start(), calls=%async_computation.8 | async-start | bytes 3145728 | tf_op jit(solution)/shard_map/all_gather | solution.py:33
  342.4 37.8 %all-to-all-start.1 = ((f32[8,256,256]{2,1,0:T(8,128)}), f32[8,256,256]{2,1,0:T(8,128)}, u32[]{:S(2)}, u32[]{:S(2)}) async-start(f32[8,256,256]{2,1,0:T(8,128)} %constant_dynamic-update-slice_fusion), calls=%async_computation.1 | async-start | bytes 4194304 | tf_op jit(solution)/shard_map/all_to_all | solution.py:93
  348.2 173.8 %all-gather.10.cloned.1.call-start = ((), (), s32[]{:S(2)}) async-start(), calls=%async_computation.6 | async-start | bytes 1064960 | tf_op jit(solution)/shard_map/all_gather | solution.py:127
  386.8 14.1 %copy-start.3 = (f32[32,256]{1,0:T(8,128)S(1)}, f32[32,256]{1,0:T(8,128)}, u32[]{:S(2)}) copy-start(f32[32,256]{1,0:T(8,128)} %param.7) | copy-start | bytes 98308
  402.9 66.6 %copy-start.1 = (f32[32,256]{1,0:T(8,128)}, f32[32,256]{1,0:T(8,128)S(1)}, u32[]{:S(2)}) copy-start(f32[32,256]{1,0:T(8,128)S(1)} %get-tuple-element.36) | copy-start | bytes 98308
  402.9 66.6 %copy-start.2 = (f32[32,256]{1,0:T(8,128)}, f32[32,256]{1,0:T(8,128)S(1)}, u32[]{:S(2)}) copy-start(f32[32,256]{1,0:T(8,128)S(1)} %get-tuple-element.24) | copy-start | bytes 98308
  403.7 64.0 %all-to-all-start.3 = ((f32[8,32,256]{2,1,0:T(8,128)}), f32[8,32,256]{2,1,0:T(8,128)S(1)}, u32[]{:S(2)}, u32[]{:S(2)}) async-start(f32[8,32,256]{2,1,0:T(8,128)} %broadcast_in_dim.4), calls=%async_computation.3 | async-start | bytes 524288 | tf_op jit(solution)/shard_map/all_to_all | solution.py:61
  469.6 13.0 %all-to-all-start.4 = ((f32[8,32,256]{2,1,0:T(8,128)}), f32[8,32,256]{2,1,0:T(8,128)S(1)}, u32[]{:S(2)}, u32[]{:S(2)}) async-start(f32[8,32,256]{2,1,0:T(8,128)} %broadcast_in_dim.5), calls=%async_computation.4 | async-start | bytes 524288 | tf_op jit(solution)/shard_map/all_to_all | solution.py:61
Sparse Core Ops, SparseCore 0:
  11.1 118.1 all-gather.7
  254.1 60.5 all-gather.11
  316.8 17.9 all-gather.13
  403.1 118.8 all-gather.9
